TPU v7x, 256 devices: a whole 4x4x8 slice. The times are simulated.
256 devices in a mesh: wide: 16 (over x_hi, z), narrow: 16 (over x_lo, y, core).
Axes of the slice: x: 4 (x_hi: 2, x_lo: 2; x = x_hi * 2 + x_lo), y: 4, z: 8, core: 2. Of those that a mesh axis runs over, the one named last changes fastest.
Arguments:
- pair_act: bfloat16 [768, 768, 128], P('wide', 'narrow'), may hold values from -6 to 6
- residue_mask: int32 [768], replicated, may hold values 0 or 1
- w_proj_start: bfloat16 [128, 512], replicated, may hold values from -0.5 to 0.5
- w_bias_start: bfloat16 [128, 4], replicated, may hold values from -40 to 40
- w_out_start: bfloat16 [128, 128], replicated, may hold values from -0.5 to 0.5
- w_proj_end: bfloat16 [128, 512], replicated, may hold values from -0.5 to 0.5
- w_bias_end: bfloat16 [128, 4], replicated, may hold values from -40 to 40
- w_out_end: bfloat16 [128, 128], replicated, may hold values from -0.5 to 0.5
Outputs:
- update_start: bfloat16 [768, 768, 128], P('wide', 'narrow')
- update_end: bfloat16 [768, 768, 128], P('wide', 'narrow')
All inputs are finite; a program needn't handle non-finite values.
Results may differ from a plain program's by a relative error of at most 0.012.
The roundings to bfloat16 on the way count: a program that leaves them out, or rounds other values in their place, can miss the bound.
Values may be sent and summed in bfloat16 or wider, within the bound.
A program may use at most 64 MiB of HBM per device.

v0:
```python
import jax
import jax.numpy as jnp
from jax import lax
from jax.sharding import Mesh
from jax.sharding import PartitionSpec as P

NARROW = ("narrow_0", "narrow_1", "narrow_2")
norm_eps = 1e-05
masked_score = -1000000000.0


def cut_along(x, dim, count):
    before, after = (x.shape[:dim], x.shape[dim + 1 :])
    return jnp.moveaxis(x.reshape(*before, count, -1, *after), dim, 0)


def in_order(parts, dim):
    parts = jnp.moveaxis(parts, 0, dim)
    shape = parts.shape
    return parts.reshape(*shape[:dim], shape[dim] * shape[dim + 1], *shape[dim + 2 :])


def turned_blocks(parts, axes, order):
    inside = parts.shape[1:]
    out = parts.reshape(*(lax.axis_size(a) for a in axes), *inside)
    for k in order:
        out = lax.all_to_all(out, axes[k], k, k, tiled=True)
    return out.reshape(-1, *inside)


def two_step_exchange(x, groups, order, split_dim, concat_dim):
    count = lax.axis_size(groups[0]) * lax.axis_size(groups[1])
    parts = cut_along(x, split_dim, count)
    return in_order(turned_blocks(parts, groups, order), concat_dim)


def layer_norm(features):
    average = jnp.mean(features, axis=-1, keepdims=True)
    centred = features - average
    spread = jnp.mean(centred * centred, axis=-1, keepdims=True)
    return (centred * lax.rsqrt(spread + norm_eps)).astype(jnp.bfloat16)


def attend(projected, pair_bias, row_ok, key_ok, head_count, head_dim):
    length = projected.shape[1]
    inv_root = head_dim ** (-0.5)

    def one_row(item_pair):
        packed, valid_row = item_pair
        packed = packed.reshape(length, head_count, 4, head_dim)
        queries = packed[:, :, 0]
        keyset = packed[:, :, 1]
        values = packed[:, :, 2]
        gating = packed[:, :, 3]
        scores = (
            jnp.einsum("bhd,khd->hbk", queries, keyset, preferred_element_type=jnp.float32)
            * inv_root
            + pair_bias
        )
        allowed = jnp.logical_and(valid_row, key_ok)
        scores = jnp.where(allowed[None, None, :], scores, masked_score)
        weights = jax.nn.softmax(scores, axis=-1).astype(jnp.bfloat16)
        summed = jnp.einsum("hbk,khd->bhd", weights, values, preferred_element_type=jnp.float32)
        gated = (jax.nn.sigmoid(gating.astype(jnp.float32)) * summed).astype(jnp.bfloat16)
        return gated.reshape(length, head_count * head_dim)

    return lax.map(one_row, (projected, row_ok))


def on_device(
    pair_act,
    residue_mask,
    w_proj_start,
    w_bias_start,
    w_out_start,
    w_proj_end,
    w_bias_end,
    w_out_end,
):
    wide_count = lax.axis_size("wide")
    narrow_count = lax.axis_size(NARROW)
    wide_at = lax.axis_index("wide")
    narrow_at = lax.axis_index(NARROW)
    tile_rows, tile_cols, channels = pair_act.shape
    head_count = w_bias_start.shape[1]
    head_dim = w_out_start.shape[0] // head_count
    residue_ok = residue_mask > 0
    normed = layer_norm(pair_act.astype(jnp.float32))
    groups = narrow_count // head_count
    sub_rows = tile_rows // groups
    proj_tile = jnp.einsum(
        "ijc,chx->hijx",
        normed,
        w_proj_start.reshape(channels, head_count, -1),
        preferred_element_type=jnp.float32,
    ).astype(jnp.bfloat16)
    outgoing = proj_tile.reshape(narrow_count, sub_rows, tile_cols, -1)
    bias_tile = jnp.einsum("ijc,ch->hij", normed, w_bias_start, preferred_element_type=jnp.float32)
    bias_out = jnp.repeat(bias_tile, groups, axis=0)
    incoming = two_step_exchange(outgoing, (("narrow_0", "narrow_1"), "narrow_2"), (1, 0), 0, 2)
    bias_rows = lax.all_to_all(bias_out, NARROW, split_axis=0, concat_axis=2, tiled=True)
    pair_bias = lax.all_gather(bias_rows, "wide", axis=1, tiled=True)
    group_at = narrow_at % groups
    first_row = wide_at * tile_rows + group_at * sub_rows
    row_ok = lax.dynamic_slice_in_dim(residue_ok, first_row, sub_rows)
    gated = attend(incoming[0], pair_bias, row_ok, residue_ok, 1, head_dim)
    returned = lax.all_to_all(
        gated.reshape(sub_rows, -1), NARROW, split_axis=1, concat_axis=0, tiled=True
    )
    head_tile = returned.reshape(head_count, tile_rows, tile_cols, head_dim)
    update_start = jnp.einsum(
        "hijd,hdc->ijc",
        head_tile,
        w_out_start.reshape(head_count, head_dim, channels),
        preferred_element_type=jnp.float32,
    ).astype(jnp.bfloat16)
    updated = pair_act.astype(jnp.float32) + update_start.astype(jnp.float32)
    normed_end = layer_norm(updated)
    groups_wide = wide_count // head_count
    sub_cols = tile_cols // groups_wide
    proj_end_tile = jnp.einsum(
        "ijc,chx->hjix",
        normed_end,
        w_proj_end.reshape(channels, head_count, -1),
        preferred_element_type=jnp.float32,
    ).astype(jnp.bfloat16)
    outgoing_end = proj_end_tile.reshape(wide_count, sub_cols, tile_rows, -1)
    bias_end_tile = jnp.einsum(
        "ijc,ch->hji", normed_end, w_bias_end, preferred_element_type=jnp.float32
    )
    bias_end_out = jnp.repeat(bias_end_tile, groups_wide, axis=0)
    incoming_end = lax.all_to_all(outgoing_end, "wide", split_axis=0, concat_axis=2, tiled=True)
    bias_cols = lax.all_to_all(bias_end_out, "wide", split_axis=0, concat_axis=2, tiled=True)
    pair_bias_end = lax.all_gather(bias_cols, NARROW, axis=1, tiled=True)
    group_wide = wide_at % groups_wide
    first_col = narrow_at * tile_cols + group_wide * sub_cols
    col_ok = lax.dynamic_slice_in_dim(residue_ok, first_col, sub_cols)
    gated_end = attend(incoming_end[0], pair_bias_end, col_ok, residue_ok, 1, head_dim)
    returned_end = lax.all_to_all(
        gated_end.reshape(sub_cols, -1), "wide", split_axis=1, concat_axis=0, tiled=True
    )
    head_tile_end = returned_end.reshape(head_count, tile_cols, tile_rows, head_dim)
    update_end = jnp.einsum(
        "hjid,hdc->ijc",
        head_tile_end,
        w_out_end.reshape(head_count, head_dim, channels),
        preferred_element_type=jnp.float32,
    ).astype(jnp.bfloat16)
    return (update_start, update_end)


def solution(mesh):
    split = Mesh(
        mesh.devices.reshape(mesh.shape["wide"], 2, 4, 2),
        ("wide", "narrow_0", "narrow_1", "narrow_2"),
    )
    placed = (P("wide", NARROW, None), P(), P(), P(), P(), P(), P(), P())
    return jax.shard_map(
        on_device,
        mesh=split,
        in_specs=placed,
        out_specs=(P("wide", NARROW, None), P("wide", NARROW, None)),
        check_vma=False,
    )
```

profile of v0, /device:TPU:40, one launch (start us, length us, event | category | flops | bytes accessed | tf_op | source)
XLA Modules:
  0.0 379.8 jit_solution(18101503657099255865)
XLA Ops:
  7.2 1.5 convert_reduce_fusion
  8.7 1.8 fusion.21
  10.5 1.9 convolution_bitcast_fusion.3
  12.9 10.5 %all_to_all.95 = f32[16,1,2304]{2,1,0:T(1,128)S(1)} all-to-all(f32[16,1,2304]{2,1,0:T(1,128)S(1)} %reshape.255), channel_id=1, replica_groups=mesh['wide'=16,'narrow_0'=2,'narrow_1'=4,'narrow_2'=2] {'narrow_0','narr..., dimensions={0} | all-to-all | bytes 294912 | tf_op jit(solution)/shard_map/all_to_all | solution.py:101
  28.3 5.6 %all_to_all.96 = bf16[8,2,1,12,48,128]{5,4,3,0,2,1:T(8,128)(2,1)S(1)} all-to-all(bf16[8,2,1,12,48,128]{5,4,3,0,2,1:T(8,128)(2,1)S(1)} %copy.76), channel_id=1, replica_groups=mesh['wide'=16,'narrow_0'=2,'narrow_1'=4,'narrow_2'=2] {'narrow_2'}, dimensions={1} | all-to-all | bytes 4718592 | tf_op jit(solution)/shard_map/all_to_all | solution.py:27
  33.9 1.8 copy.77
  35.7 5.8 %all-to-all-start.1 = ((bf16[8,2,1,12,48,128]{5,4,3,1,2,0:T(8,128)(2,1)}), bf16[8,2,1,12,48,128]{5,4,3,1,2,0:T(8,128)(2,1)S(1)}, u32[]{:S(2)}, u32[]{:S(2)}) async-start(bf16[8,2,1,12,48,128]{5,4,3,1,2,0:T(8,128)(2,1)} %copy.77), calls=%async_computation.1 | async-start | bytes 4718592 | tf_op jit(solution)/shard_map/all_to_all | solution.py:27
  41.6 28.6 %all-to-all-done.1 = bf16[8,2,1,12,48,128]{5,4,3,1,2,0:T(8,128)(2,1)S(1)} async-done(((bf16[8,2,1,12,48,128]{5,4,3,1,2,0:T(8,128)(2,1)}), bf16[8,2,1,12,48,128]{5,4,3,1,2,0:T(8,128)(2,1)S(1)}, u32[]{:S(2)}, u32[]{:S(2)}) %all-to-all-start.1) | async-done | bytes 2359328 | tf_op jit(solution)/shard_map/all_to_all | solution.py:27
  70.2 2.0 copy.78
  72.2 43.2 %all-gather.3.cloned.1.call-done = f32[1,768,768]{2,0,1:T(1,128)} async-done(((f32[1,48,768]{2,0,1:T(1,128)}), f32[1,768,768]{2,0,1:T(1,128)}) %all-gather.3.cloned.1.call-update) | async-done | bytes 2359312 | tf_op jit(solution)/shard_map/all_gather | solution.py:102
  115.4 5.5 %copy.83 = f32[1,768,768]{1,2,0:T(8,128)S(1)} copy(f32[1,768,768]{2,0,1:T(1,128)} %all-gather.3.cloned.1.call-done) | data formatting | bytes 4718592 | tf_op jit(solution)/shard_map/while | solution.py:67
  121.8 52.3 %while.20 = (s32[]{:T(128)}, bf16[12,768,32]{1,2,0:T(8,128)(2,1)}, bf16[12,768,128]{2,1,0:T(8,128)(2,1)}, pred[12]{0:T(512)(128)(4,1)S(1)}, pred[768]{0:T(1024)(...) while((s32[]{:T(128)}, bf16[12,768,32]{1,2,0:T(8,128)(2,1)}, bf16[12,768,128]{2,1,0:T(8,128)(2,1)}, ...), condition=%wide.region_5.6_spmd, body=%wide.region_2.5_spmd.sunk | while | flops 80952576 | bytes 10489944 | solution.py:67
  129.3 1.1 fusion.50
  174.1 2.0 copy.84
  176.1 3.0 all_to_all.73
  179.2 1.4 copy.85
  180.6 15.9 %all_to_all.97 = bf16[12,16,1536]{2,0,1:T(8,128)(2,1)} all-to-all(bf16[12,16,1536]{2,0,1:T(8,128)(2,1)S(1)} %copy.85), channel_id=1, replica_groups=mesh['wide'=16,'narrow_0'=2,'narrow_1'=4,'narrow_2'=2] {'narrow_0','narr..., dimensions={1} | all-to-all | bytes 1179648 | tf_op jit(solution)/shard_map/all_to_all | solution.py:107
  196.5 3.0 reshape.234
  199.5 1.4 fusion.24
  203.9 6.7 %all-to-all-start.5 = ((f32[16,1,2304]{2,1,0:T(1,128)}), f32[16,1,2304]{2,1,0:T(1,128)S(1)}, u32[]{:S(2)}, u32[]{:S(2)}) async-start(f32[16,1,2304]{2,1,0:T(1,128)} %reshape.257), calls=%async_computation.5 | async-start | bytes 294912 | tf_op jit(solution)/shard_map/all_to_all | solution.py:133
  210.6 1.9 convert_bitcast_fusion
  212.5 2.9 copy.88
  215.5 5.7 %all-to-all-done.5 = f32[16,1,2304]{2,1,0:T(1,128)S(1)} async-done(((f32[16,1,2304]{2,1,0:T(1,128)}), f32[16,1,2304]{2,1,0:T(1,128)S(1)}, u32[]{:S(2)}, u32[]{:S(2)}) %all-to-all-start.5) | async-done | bytes 147488 | tf_op jit(solution)/shard_map/all_to_all | solution.py:133
  221.2 4.0 %all-to-all-start.4 = ((bf16[16,12,48,128]{3,2,1,0:T(8,128)(2,1)}), bf16[16,12,48,128]{3,2,1,0:T(8,128)(2,1)S(1)}, u32[]{:S(2)}, u32[]{:S(2)}) async-start(bf16[16,12,48,128]{3,2,1,0:T(8,128)(2,1)} %bitcast.42), calls=%async_computation.4 | async-start | bytes 4718592 | tf_op jit(solution)/shard_map/all_to_all | solution.py:132
  227.9 52.0 %all-to-all-done.4 = bf16[16,12,48,128]{3,2,1,0:T(8,128)(2,1)S(1)} async-done(((bf16[16,12,48,128]{3,2,1,0:T(8,128)(2,1)}), bf16[16,12,48,128]{3,2,1,0:T(8,128)(2,1)S(1)}, u32[]{:S(2)}, u32[]{:S(2)}) %all-to-all-start.4) | async-done | bytes 2359328 | tf_op jit(solution)/shard_map/all_to_all | solution.py:132
  279.9 2.0 copy.89
  281.9 5.5 %copy.94 = f32[1,768,768]{1,2,0:T(8,128)S(1)} copy(f32[1,768,768]{2,0,1:T(1,128)} %all-gather.5.cloned.1.call-done) | data formatting | bytes 4718592 | tf_op jit(solution)/shard_map/while | solution.py:67
  287.4 46.0 %while.21 = (s32[]{:T(128)}, bf16[12,768,32]{1,2,0:T(8,128)(2,1)S(1)}, bf16[12,768,128]{2,1,0:T(8,128)(2,1)}, pred[12]{0:T(512)(128)(4,1)S(1)}, pred[768]{0:T(10...) while((s32[]{:T(128)}, bf16[12,768,32]{1,2,0:T(8,128)(2,1)S(1)}, ...), condition=%wide.region_11.12_spmd, body=%wide.region_8.11_spmd.sunk | while | flops 80952576 | bytes 10489436 | solution.py:67
  333.5 1.1 copy.95
  334.6 2.3 all_to_all.83
  337.3 32.0 %all_to_all.98 = bf16[12,16,1536]{2,0,1:T(8,128)(2,1)S(1)} all-to-all(bf16[12,16,1536]{2,0,1:T(8,128)(2,1)S(1)} %copy.96), channel_id=1, replica_groups=mesh['wide'=16,'narrow_0'=2,'narrow_1'=4,'narrow_2'=2] {'wide'}, dimensions={1} | all-to-all | bytes 1179648 | tf_op jit(solution)/shard_map/all_to_all | solution.py:139
  369.3 1.6 reshape.239
  (219 shorter events, 111.0 us)
Async XLA Ops:
  7.2 19.2 %copy-start = (bf16[128,512]{1,0:T(8,128)(2,1)S(1)}, bf16[128,512]{1,0:T(8,128)(2,1)}, u32[]{:S(2)}) copy-start(bf16[128,512]{1,0:T(8,128)(2,1)} %param.14) | copy-start | bytes 393220
  7.2 108.2 %all-gather.3.cloned.1.call-start = ((), (), s32[]{:S(2)}) async-start(), calls=%async_computation.7 | async-start | bytes 2506752 | tf_op jit(solution)/shard_map/all_gather | solution.py:102
  10.5 15.9 %copy-start.1 = (bf16[48,48,128]{2,1,0:T(8,128)(2,1)S(1)}, bf16[48,48,128]{2,1,0:T(8,128)(2,1)}, u32[]{:S(2)}) copy-start(bf16[48,48,128]{2,1,0:T(8,128)(2,1)} %param.12) | copy-start | bytes 1769476
  35.7 5.8 %copy-start.6 = (s32[768]{0:T(1024)S(1)}, s32[768]{0:T(1024)}, u32[]{:S(2)}) copy-start(s32[768]{0:T(1024)} %param.13) | copy-start | bytes 9220
  35.7 34.5 %all-to-all-start.1 = ((bf16[8,2,1,12,48,128]{5,4,3,1,2,0:T(8,128)(2,1)}), bf16[8,2,1,12,48,128]{5,4,3,1,2,0:T(8,128)(2,1)S(1)}, u32[]{:S(2)}, u32[]{:S(2)}) async-start(bf16[8,2,1,12,48,128]{5,4,3,1,2,0:T(8,128)(2,1)} %copy.77), calls=%async_computation.1 | async-start | bytes 4718592 | tf_op jit(solution)/shard_map/all_to_all | solution.py:27
  180.6 18.9 %copy-start.4 = (bf16[128,128]{1,0:T(8,128)(2,1)S(1)}, bf16[128,128]{1,0:T(8,128)(2,1)}, u32[]{:S(2)}) copy-start(bf16[128,128]{1,0:T(8,128)(2,1)} %param.16) | copy-start | bytes 98308
  199.4 2.3 copy-start.7
  200.9 0.8 copy-start.2
  200.9 9.7 %copy-start.3 = (bf16[128,512]{1,0:T(8,128)(2,1)S(1)}, bf16[128,512]{1,0:T(8,128)(2,1)}, u32[]{:S(2)}) copy-start(bf16[128,512]{1,0:T(8,128)(2,1)} %param.17) | copy-start | bytes 393220
  203.9 17.3 %all-to-all-start.5 = ((f32[16,1,2304]{2,1,0:T(1,128)}), f32[16,1,2304]{2,1,0:T(1,128)S(1)}, u32[]{:S(2)}, u32[]{:S(2)}) async-start(f32[16,1,2304]{2,1,0:T(1,128)} %reshape.257), calls=%async_computation.5 | async-start | bytes 294912 | tf_op jit(solution)/shard_map/all_to_all | solution.py:133
  221.2 58.7 %all-to-all-start.4 = ((bf16[16,12,48,128]{3,2,1,0:T(8,128)(2,1)}), bf16[16,12,48,128]{3,2,1,0:T(8,128)(2,1)S(1)}, u32[]{:S(2)}, u32[]{:S(2)}) async-start(bf16[16,12,48,128]{3,2,1,0:T(8,128)(2,1)} %bitcast.42), calls=%async_computation.4 | async-start | bytes 4718592 | tf_op jit(solution)/shard_map/all_to_all | solution.py:132
  225.2 56.7 %all-gather.5.cloned.1.call-start = ((), (), s32[]{:S(2)}) async-start(), calls=%async_computation.8 | async-start | bytes 2506752 | tf_op jit(solution)/shard_map/all_gather | solution.py:134
  337.3 33.6 %copy-start.5 = (bf16[128,128]{1,0:T(8,128)(2,1)S(1)}, bf16[128,128]{1,0:T(8,128)(2,1)}, u32[]{:S(2)}) copy-start(bf16[128,128]{1,0:T(8,128)(2,1)} %param.19) | copy-start | bytes 98308
Sparse Core Ops, SparseCore 0:
  26.5 88.9 all-gather.2
  228.5 46.1 all-gather.4
where the time goes:
time: 382 us; the launch traced here: 380 us
  waiting for transfers between devices  130 us (34%)
  local copies, waits for them, and re-layouts  82.4 us (22%)
  blocking collectives  64 us (17%)
  matrix products  42.6 us (11%)
  other arithmetic  29.4 us (8%)
  starting transfers between devices  16.8 us (4%)
  between operations  14.4 us (4%)
    all_to_all x1, waiting for transfers between devices, on_device(): lax.all_to_all(outgoing_end, 'wide', split_axis=0, concat_axis=2, tiled=T...  52 us
    all_gather x1, waiting for transfers between devices, on_device(): pair_bias = lax.all_gather(bias_rows, 'wide', axis=1, tiled=True)  43.2 us
    dynamic_slice x72, local copies, waits for them, and re-layouts, attend(): return lax.map(one_row, (projected, row_ok))  40.2 us
    all_to_all x1, blocking collectives, on_device(): lax.all_to_all(gated_end.reshape(sub_cols, -1), 'wide', split_axis=1, con...  32 us
    all_to_all x1, waiting for transfers between devices, turned_blocks(): out = lax.all_to_all(out, axes[k], k, k, tiled=True)  28.6 us
    dot_general x24, matrix products, one_row(): jnp.einsum('hbk,khd->bhd', weights, values, preferred_element_type=jnp.fl...  19.8 us
    all_to_all x1, blocking collectives, on_device(): lax.all_to_all(gated.reshape(sub_rows, -1), NARROW, split_axis=1, concat_...  15.9 us
    and x24, other arithmetic, one_row(): allowed = jnp.logical_and(valid_row, key_ok)  14.6 us
  transfers between devices with their start and end apart: 5, of which 4 were waited for; matrix products, arithmetic and copies ran while one was open for 4% of the time, Pallas kernels for 0%

commit v1 on v0

--- a/solution.py
+++ b/solution.py
@@ -99,7 +99,9 @@
     bias_out = jnp.repeat(bias_tile, groups, axis=0)
     incoming = two_step_exchange(outgoing, (("narrow_0", "narrow_1"), "narrow_2"), (1, 0), 0, 2)
     bias_rows = lax.all_to_all(bias_out, NARROW, split_axis=0, concat_axis=2, tiled=True)
-    pair_bias = lax.all_gather(bias_rows, "wide", axis=1, tiled=True)
+    pair_bias = jnp.concatenate(
+        lax.all_to_all(jnp.stack(lax.axis_size("wide") * [bias_rows]), "wide", 0, 0), axis=1
+    )
     group_at = narrow_at % groups
     first_row = wide_at * tile_rows + group_at * sub_rows
     row_ok = lax.dynamic_slice_in_dim(residue_ok, first_row, sub_rows)

time: 382 us -> 410 us (1.073)
  starting transfers between devices: 16.8 us -> 39.3 us
  blocking collectives: 64 us -> 48.1 us
  matrix products: 42.6 us -> 50 us
  waiting for transfers between devices: 130 us -> 137 us
  local copies, waits for them, and re-layouts: 82.4 us -> 87.8 us
    all_to_all x0 -> x2, waiting for transfers between devices: none -> 55.5 us  [the longest x1 52.5 us: on_device(): lax.all_to_all(jnp.stack(lax.axis_size('wide') * [bias_rows]), 'wide', 0, 0)]
    all_gather x1 -> x0, waiting for transfers between devices: 43.2 us -> none  [on_device(): pair_bias = lax.all_gather(bias_rows, 'wide', axis=1, tiled=True)]
    all_to_all x0 -> x2, starting transfers between devices: none -> 16.7 us  [the longest x1 10.9 us: on_device(): lax.all_to_all(jnp.stack(lax.axis_size('wide') * [bias_rows]), 'wide', 0, 0)]
    all_to_all x2 -> x0, blocking collectives: 16.1 us -> none  [the longest x1 10.5 us: on_device(): lax.all_to_all(bias_out, NARROW, split_axis=0, concat_axis=2, tiled=True)]
    dot_general x24, matrix products: 19.8 us -> 27.3 us  [one_row(): jnp.einsum('hbk,khd->bhd', weights, values, preferred_element_type=jnp.fl...]
    all_to_all x1 -> x2, waiting for transfers between devices: 28.6 us -> 23.6 us  [turned_blocks(): out = lax.all_to_all(out, axes[k], k, k, tiled=True)]
    all_to_all x1 -> x2, starting transfers between devices: 5.82 us -> 9.63 us  [turned_blocks(): out = lax.all_to_all(out, axes[k], k, k, tiled=True)]
  transfers between devices with their start and end apart: 5 -> 7, of which waited for: 4 -> 6; matrix products, arithmetic and copies ran while one was open for 4% -> 5% of each run, Pallas kernels for 0% -> 0%
where the time goes in v1:
time: 410 us; the launch traced here: 408 us
  waiting for transfers between devices  137 us (33%)
  local copies, waits for them, and re-layouts  87.8 us (21%)
  matrix products  50 us (12%)
  blocking collectives  48.1 us (12%)
  starting transfers between devices  39.3 us (10%)
  other arithmetic  30.5 us (7%)
  between operations  14.4 us (4%)
    all_to_all x1, waiting for transfers between devices, on_device(): lax.all_to_all(jnp.stack(lax.axis_size('wide') * [bias_rows]), 'wide', 0, 0)  52.5 us
    all_to_all x1, waiting for transfers between devices, on_device(): lax.all_to_all(outgoing_end, 'wide', split_axis=0, concat_axis=2, tiled=T...  52.1 us
    dynamic_slice x72, local copies, waits for them, and re-layouts, attend(): return lax.map(one_row, (projected, row_ok))  40.5 us
    all_to_all x1, blocking collectives, on_device(): lax.all_to_all(gated_end.reshape(sub_cols, -1), 'wide', split_axis=1, con...  32 us
    dot_general x24, matrix products, one_row(): jnp.einsum('hbk,khd->bhd', weights, values, preferred_element_type=jnp.fl...  27.3 us
    all_to_all x2, waiting for transfers between devices, turned_blocks(): out = lax.all_to_all(out, axes[k], k, k, tiled=True)  23.6 us
    all_to_all x1, blocking collectives, on_device(): lax.all_to_all(gated.reshape(sub_rows, -1), NARROW, split_axis=1, concat_...  16.1 us
    and x24, other arithmetic, one_row(): allowed = jnp.logical_and(valid_row, key_ok)  15.1 us
  transfers between devices with their start and end apart: 7, of which 6 were waited for; matrix products, arithmetic and copies ran while one was open for 5% of the time, Pallas kernels for 0%

profile of v1, /device:TPU:40, one launch (start us, length us, event | category | flops | bytes accessed | tf_op | source)
XLA Modules:
  0.0 407.6 jit_solution(3901342508315159450)
XLA Ops:
  8.7 1.8 fusion.21
  10.5 1.9 convert_bitcast_fusion.1
  12.8 1.8 copy.100
  14.6 3.9 all-to-all-start
  21.6 5.9 %all-to-all-start.2 = ((f32[16,1,2304]{2,1,0:T(1,128)}), f32[16,1,2304]{2,1,0:T(1,128)S(1)}, u32[]{:S(2)}, u32[]{:S(2)}) async-start(f32[16,1,2304]{2,1,0:T(1,128)} %reshape.264), calls=%async_computation.2 | async-start | bytes 294912 | tf_op jit(solution)/shard_map/all_to_all | solution.py:101
  27.4 1.8 copy.101
  29.3 3.0 all-to-all-done.2
  32.3 5.7 %all-to-all-start.1 = ((bf16[8,2,1,12,48,128]{5,4,3,1,2,0:T(8,128)(2,1)}), bf16[8,2,1,12,48,128]{5,4,3,1,2,0:T(8,128)(2,1)S(1)}, u32[]{:S(2)}, u32[]{:S(2)}) async-start(bf16[8,2,1,12,48,128]{5,4,3,1,2,0:T(8,128)(2,1)} %copy.101), calls=%async_computation.1 | async-start | bytes 4718592 | tf_op jit(solution)/shard_map/all_to_all | solution.py:27
  43.2 22.7 %all-to-all-done.1 = bf16[8,2,1,12,48,128]{5,4,3,1,2,0:T(8,128)(2,1)S(1)} async-done(((bf16[8,2,1,12,48,128]{5,4,3,1,2,0:T(8,128)(2,1)}), bf16[8,2,1,12,48,128]{5,4,3,1,2,0:T(8,128)(2,1)S(1)}, u32[]{:S(2)}, u32[]{:S(2)}) %all-to-all-start.1) | async-done | bytes 2359328 | tf_op jit(solution)/shard_map/all_to_all | solution.py:27
  65.9 1.7 stack.5
  67.6 10.9 %all-to-all-start.3 = ((f32[16,1,48,768]{3,2,1,0:T(8,128)}), f32[16,1,48,768]{3,2,1,0:T(8,128)}, u32[]{:S(2)}, u32[]{:S(2)}) async-start(f32[16,1,48,768]{3,2,1,0:T(8,128)} %stack.5), calls=%async_computation.3 | async-start | bytes 4718592 | tf_op jit(solution)/shard_map/all_to_all | solution.py:103
  78.6 2.0 copy.102
  80.6 52.5 %all-to-all-done.3 = f32[16,1,48,768]{3,2,1,0:T(8,128)} async-done(((f32[16,1,48,768]{3,2,1,0:T(8,128)}), f32[16,1,48,768]{3,2,1,0:T(8,128)}, u32[]{:S(2)}, u32[]{:S(2)}) %all-to-all-start.3) | async-done | bytes 2359328 | tf_op jit(solution)/shard_map/all_to_all | solution.py:103
  133.0 2.0 copy.106
  135.9 53.3 %while.20 = (s32[]{:T(128)}, bf16[12,768,32]{1,2,0:T(8,128)(2,1)}, bf16[12,768,128]{2,1,0:T(8,128)(2,1)}, pred[12]{0:T(512)(128)(4,1)S(1)}, pred[768]{0:T(1024)(...) while((s32[]{:T(128)}, bf16[12,768,32]{1,2,0:T(8,128)(2,1)}, bf16[12,768,128]{2,1,0:T(8,128)(2,1)}, ...), condition=%wide.region_5.6_spmd, body=%wide.region_2.5_spmd.sunk | while | flops 80952576 | bytes 10489944 | solution.py:67
  189.2 2.0 copy.107
  191.3 3.0 all_to_all.74
  195.8 16.1 %all_to_all.96 = bf16[12,16,1536]{2,0,1:T(8,128)(2,1)} all-to-all(bf16[12,16,1536]{2,0,1:T(8,128)(2,1)S(1)} %copy.108), channel_id=1, replica_groups=mesh['wide'=16,'narrow_0'=2,'narrow_1'=4,'narrow_2'=2] {'narrow_0','narr..., dimensions={1} | all-to-all | bytes 1179648 | tf_op jit(solution)/shard_map/all_to_all | solution.py:109
  211.8 3.0 reshape.243
  219.3 8.7 %all-to-all-start.6 = ((f32[16,1,2304]{2,1,0:T(1,128)}), f32[16,1,2304]{2,1,0:T(1,128)S(1)}, u32[]{:S(2)}, u32[]{:S(2)}) async-start(f32[16,1,2304]{2,1,0:T(1,128)} %reshape.266), calls=%async_computation.6 | async-start | bytes 294912 | tf_op jit(solution)/shard_map/all_to_all | solution.py:135
  227.9 1.9 convert_bitcast_fusion
  229.8 2.9 copy.111
  232.8 5.7 %all-to-all-done.6 = f32[16,1,2304]{2,1,0:T(1,128)S(1)} async-done(((f32[16,1,2304]{2,1,0:T(1,128)}), f32[16,1,2304]{2,1,0:T(1,128)S(1)}, u32[]{:S(2)}, u32[]{:S(2)}) %all-to-all-start.6) | async-done | bytes 147488 | tf_op jit(solution)/shard_map/all_to_all | solution.py:135
  238.5 4.0 all-to-all-start.5
  245.1 52.1 %all-to-all-done.5 = bf16[16,12,48,128]{3,2,1,0:T(8,128)(2,1)S(1)} async-done(((bf16[16,12,48,128]{3,2,1,0:T(8,128)(2,1)}), bf16[16,12,48,128]{3,2,1,0:T(8,128)(2,1)S(1)}, u32[]{:S(2)}, u32[]{:S(2)}) %all-to-all-start.5) | async-done | bytes 2359328 | tf_op jit(solution)/shard_map/all_to_all | solution.py:134
  297.2 2.0 copy.112
  299.2 5.5 %copy.117 = f32[1,768,768]{1,2,0:T(8,128)S(1)} copy(f32[1,768,768]{2,0,1:T(1,128)} %all-gather.2.cloned.1.call-done) | data formatting | bytes 4718592 | tf_op jit(solution)/shard_map/while | solution.py:67
  305.6 53.3 %while.21 = (s32[]{:T(128)}, bf16[12,768,32]{1,2,0:T(8,128)(2,1)}, bf16[12,768,128]{2,1,0:T(8,128)(2,1)}, pred[12]{0:T(512)(128)(4,1)S(1)}, pred[768]{0:T(1024)(...) while((s32[]{:T(128)}, bf16[12,768,32]{1,2,0:T(8,128)(2,1)}, bf16[12,768,128]{2,1,0:T(8,128)(2,1)}, ...), condition=%wide.region_11.12_spmd, body=%wide.region_8.11_spmd.sunk | while | flops 80952576 | bytes 10489944 | solution.py:67
  358.9 2.0 copy.118
  361.0 2.3 all_to_all.84
  363.6 32.0 %all_to_all.97 = bf16[12,16,1536]{2,0,1:T(8,128)(2,1)} all-to-all(bf16[12,16,1536]{2,0,1:T(8,128)(2,1)S(1)} %copy.119), channel_id=1, replica_groups=mesh['wide'=16,'narrow_0'=2,'narrow_1'=4,'narrow_2'=2] {'wide'}, dimensions={1} | all-to-all | bytes 1179648 | tf_op jit(solution)/shard_map/all_to_all | solution.py:141
  395.7 3.0 reshape.248
  (223 shorter events, 128.9 us)
Async XLA Ops:
  7.2 3.3 copy-start
  14.6 4.0 copy-start.1
  14.6 4.0 copy-start.7
  14.6 7.0 %all-to-all-start = ((bf16[8,2,1,12,48,128]{5,4,3,0,2,1:T(8,128)(2,1)}), bf16[8,2,1,12,48,128]{5,4,3,0,2,1:T(8,128)(2,1)S(1)}, u32[]{:S(2)}, u32[]{:S(2)}) async-start(bf16[8,2,1,12,48,128]{5,4,3,0,2,1:T(8,128)(2,1)} %copy.100), calls=%async_computation | async-start | bytes 4718592 | tf_op jit(solution)/shard_map/all_to_all | solution.py:27
  21.6 10.7 %all-to-all-start.2 = ((f32[16,1,2304]{2,1,0:T(1,128)}), f32[16,1,2304]{2,1,0:T(1,128)S(1)}, u32[]{:S(2)}, u32[]{:S(2)}) async-start(f32[16,1,2304]{2,1,0:T(1,128)} %reshape.264), calls=%async_computation.2 | async-start | bytes 294912 | tf_op jit(solution)/shard_map/all_to_all | solution.py:101
  32.3 33.6 %all-to-all-start.1 = ((bf16[8,2,1,12,48,128]{5,4,3,1,2,0:T(8,128)(2,1)}), bf16[8,2,1,12,48,128]{5,4,3,1,2,0:T(8,128)(2,1)S(1)}, u32[]{:S(2)}, u32[]{:S(2)}) async-start(bf16[8,2,1,12,48,128]{5,4,3,1,2,0:T(8,128)(2,1)} %copy.101), calls=%async_computation.1 | async-start | bytes 4718592 | tf_op jit(solution)/shard_map/all_to_all | solution.py:27
  67.6 10.9 %copy-start.6 = (s32[768]{0:T(1024)S(1)}, s32[768]{0:T(1024)}, u32[]{:S(2)}) copy-start(s32[768]{0:T(1024)} %param.13) | copy-start | bytes 9220
  67.6 65.4 %all-to-all-start.3 = ((f32[16,1,48,768]{3,2,1,0:T(8,128)}), f32[16,1,48,768]{3,2,1,0:T(8,128)}, u32[]{:S(2)}, u32[]{:S(2)}) async-start(f32[16,1,48,768]{3,2,1,0:T(8,128)} %stack.5), calls=%async_computation.3 | async-start | bytes 4718592 | tf_op jit(solution)/shard_map/all_to_all | solution.py:103
  195.7 19.1 %copy-start.4 = (bf16[128,128]{1,0:T(8,128)(2,1)S(1)}, bf16[128,128]{1,0:T(8,128)(2,1)}, u32[]{:S(2)}) copy-start(bf16[128,128]{1,0:T(8,128)(2,1)} %param.16) | copy-start | bytes 98308
  214.8 2.3 copy-start.8
  216.2 0.8 copy-start.2
  216.3 11.7 %copy-start.3 = (bf16[128,512]{1,0:T(8,128)(2,1)S(1)}, bf16[128,512]{1,0:T(8,128)(2,1)}, u32[]{:S(2)}) copy-start(bf16[128,512]{1,0:T(8,128)(2,1)} %param.17) | copy-start | bytes 393220
  219.3 19.2 %all-to-all-start.6 = ((f32[16,1,2304]{2,1,0:T(1,128)}), f32[16,1,2304]{2,1,0:T(1,128)S(1)}, u32[]{:S(2)}, u32[]{:S(2)}) async-start(f32[16,1,2304]{2,1,0:T(1,128)} %reshape.266), calls=%async_computation.6 | async-start | bytes 294912 | tf_op jit(solution)/shard_map/all_to_all | solution.py:135
  238.5 58.7 %all-to-all-start.5 = ((bf16[16,12,48,128]{3,2,1,0:T(8,128)(2,1)}), bf16[16,12,48,128]{3,2,1,0:T(8,128)(2,1)S(1)}, u32[]{:S(2)}, u32[]{:S(2)}) async-start(bf16[16,12,48,128]{3,2,1,0:T(8,128)(2,1)} %bitcast.43), calls=%async_computation.5 | async-start | bytes 4718592 | tf_op jit(solution)/shard_map/all_to_all | solution.py:134
  242.5 56.7 %all-gather.2.cloned.1.call-start = ((), (), s32[]{:S(2)}) async-start(), calls=%async_computation.8 | async-start | bytes 2506752 | tf_op jit(solution)/shard_map/all_gather | solution.py:136
  363.6 35.0 %copy-start.5 = (bf16[128,128]{1,0:T(8,128)(2,1)S(1)}, bf16[128,128]{1,0:T(8,128)(2,1)}, u32[]{:S(2)}) copy-start(bf16[128,128]{1,0:T(8,128)(2,1)} %param.19) | copy-start | bytes 98308
Sparse Core Ops, SparseCore 0:
  245.8 46.1 all-gather.1
